TPU v7x, 32 devices: a whole 2x2x4 slice. The times are simulated.
32 devices in a mesh: role: 4 (over z), seq: 2 (over y), tp: 4 (over x, core).
Axes of the slice: x: 2, y: 2, z: 4, core: 2. Of those that a mesh axis runs over, the one named last changes fastest.
Arguments:
- teacher_rows: bfloat16 [4, 1024, 8192], P('role', 'seq', 'tp'), may hold values from -16 to 16
- teacher_gain: float32 [8192], P('tp'), may hold values from 0.5 to 1.5
- proj: bfloat16 [8192, 4096], P('tp', 'seq'), may hold values from -0.0625 to 0.0625
- streams: bfloat16 [4, 1024, 4, 4096], P('role', 'seq', None, 'tp'), may hold values from -5 to 5
- hc_read: float32 [4], replicated, may hold values from 0.5 to 1.5
- hc_mix: float32 [4, 4], replicated, may hold values from -3 to 3
- hc_write: float32 [4], replicated, may hold values from 0.5 to 1.5
- norm_gain: float32 [4096], P('tp'), may hold values from 0.5 to 1.5
- w_query: bfloat16 [4096, 4096], P('seq', 'tp'), may hold values from -0.09375 to 0.09375
- w_kv: bfloat16 [4096, 2048], P('tp'), may hold values from -0.09375 to 0.09375
- w_out: bfloat16 [4096, 4096], P('tp', 'seq'), may hold values from -0.09375 to 0.09375
Outputs:
- grad_streams: bfloat16 [4, 1024, 4, 4096], P('role', 'seq', None, 'tp')
- loss_value: float32 [], replicated
All inputs are finite; a program needn't handle non-finite values.
Results may differ from a plain program's by a relative error of at most 0.024.
Values may be sent and summed in bfloat16 or wider, within the bound.
A program may use at most 192 MiB of HBM per device.

v0:
```python
import jax
import jax.numpy as jnp
from jax import lax
from jax.sharding import PartitionSpec as P

HEADS = 32
KVH = 8
HD = 128


epsilon = 1e-05


def per_device(
    teacher_rows,
    teacher_gain,
    proj,
    streams,
    hc_read,
    hc_mix,
    hc_write,
    norm_gain,
    w_query,
    w_kv,
    w_out,
):
    f32 = jnp.float32
    bf16 = jnp.bfloat16
    n_tp = lax.axis_size("tp")
    tp_index = lax.axis_index("tp")
    seq_index = lax.axis_index("seq")
    teacher = teacher_rows[0].astype(f32)
    hidden = streams[0].astype(f32)
    mixed_in = jnp.sum(hidden * hc_read[None, :, None], axis=1)
    feat_block = mixed_in.shape[1]
    teacher_sq, student_sq = lax.psum(
        (jnp.sum(teacher * teacher, axis=1), jnp.sum(mixed_in * mixed_in, axis=1)), "tp"
    )
    inv_t = lax.rsqrt(teacher_sq / (teacher.shape[1] * n_tp) + epsilon)
    normed_t = (teacher * inv_t[:, None] * teacher_gain[None, :]).astype(bf16)
    local_len = normed_t.shape[0]
    proj_full = lax.all_gather(proj, "seq", axis=1, tiled=True)
    target_term = jnp.dot(normed_t, proj_full, preferred_element_type=f32)
    target = lax.psum_scatter(
        target_term.astype(jnp.bfloat16), "tp", scatter_dimension=1, tiled=True
    ).astype(jnp.float32)
    inv_rms = lax.rsqrt(student_sq / (feat_block * n_tp) + epsilon)
    normed_s = (mixed_in * inv_rms[:, None] * norm_gain[None, :]).astype(bf16)
    heads_dev = w_query.shape[1] // HD
    group = HEADS // KVH
    kv_dev = max(1, heads_dev // group)
    per_kv = heads_dev // kv_dev
    ratio = max(1, group // heads_dev)
    first = tp_index * heads_dev // group
    query_full = lax.all_gather(w_query, "seq", axis=0, tiled=True)
    kv_part = jnp.dot(normed_s, w_kv, preferred_element_type=f32)
    kv_all = lax.psum(kv_part.astype(jnp.bfloat16), "tp").astype(jnp.float32).astype(bf16)
    keys_own = lax.dynamic_slice_in_dim(kv_all, first * HD, kv_dev * HD, 1)
    vals_own = lax.dynamic_slice_in_dim(kv_all, (KVH + first) * HD, kv_dev * HD, 1)
    rows_full = lax.all_gather(normed_s, "tp", axis=1, tiled=True)
    query = jnp.dot(rows_full, query_full, preferred_element_type=f32).astype(bf16)
    keys_all, vals_all = (
        lax.all_gather(keys_own, "seq", axis=0, tiled=True),
        lax.all_gather(vals_own, "seq", axis=0, tiled=True),
    )
    whole_len = keys_all.shape[0]
    scale = HD ** (-0.5)
    query4 = query.reshape(local_len, kv_dev, per_kv, HD)
    keys3 = keys_all.reshape(whole_len, kv_dev, HD)
    vals3 = vals_all.reshape(whole_len, kv_dev, HD)
    scores = jnp.einsum("qgjd,kgd->gjqk", query4, keys3, preferred_element_type=f32) * scale
    query_pos = seq_index * local_len + lax.iota(jnp.int32, local_len)
    key_pos = lax.iota(jnp.int32, whole_len)
    allowed = key_pos[None, :] <= query_pos[:, None]
    scores = jnp.where(allowed, scores, -1e30)
    expo = jnp.exp(scores)
    probs = expo / jnp.sum(expo, axis=-1, keepdims=True)
    probs_low = probs.astype(bf16)
    attended = jnp.einsum("gjqk,kgd->qgjd", probs_low, vals3, preferred_element_type=f32).astype(
        bf16
    )
    attended = attended.reshape(local_len, heads_dev * HD)
    out_full = lax.all_gather(w_out, "seq", axis=1, tiled=True)
    out_term = jnp.dot(attended, out_full, preferred_element_type=f32)
    layer_out = lax.psum_scatter(
        out_term.astype(jnp.bfloat16), "tp", scatter_dimension=1, tiled=True
    ).astype(jnp.float32)
    carry = jnp.sum(hc_mix, axis=0)
    write = jnp.sum(hc_write)
    student = jnp.sum(hidden * carry[None, :, None], axis=1) + write * layer_out
    error = student - target
    loss_total = lax.psum(jnp.sum(error * error), ("role", "seq", "tp"))
    loss_value = loss_total / (lax.axis_size("role") * whole_len * feat_block * n_tp)
    grad_out = (write * error).astype(bf16)
    grad_full = lax.all_gather(grad_out, "tp", axis=1, tiled=True)
    grad_att = lax.dot_general(
        grad_full, out_full, (((1,), (1,)), ((), ())), preferred_element_type=f32
    ).astype(bf16)
    grad4 = grad_att.reshape(local_len, kv_dev, per_kv, HD)
    att4 = attended.reshape(local_len, kv_dev, per_kv, HD)
    grad_probs = jnp.einsum("qgjd,kgd->gjqk", grad4, vals3, preferred_element_type=f32)
    delta = jnp.einsum("qgjd,qgjd->gjq", grad4, att4, preferred_element_type=f32)
    grad_scores = (probs * (grad_probs - delta[..., None])).astype(bf16)
    grad_query = (
        jnp.einsum("gjqk,kgd->qgjd", grad_scores, keys3, preferred_element_type=f32) * scale
    ).astype(bf16)
    grad_query = grad_query.reshape(local_len, heads_dev * HD)
    grad_keys = (
        jnp.einsum("gjqk,qgjd->kgd", grad_scores, query4, preferred_element_type=f32) * scale
    )
    grad_vals = jnp.einsum("gjqk,qgjd->kgd", probs_low, grad4, preferred_element_type=f32)
    key_sum, val_sum = (
        lax.psum_scatter(
            grad_keys.reshape(whole_len, kv_dev * HD).astype(jnp.bfloat16),
            "seq",
            scatter_dimension=0,
            tiled=True,
        ).astype(jnp.float32),
        lax.psum_scatter(
            grad_vals.reshape(whole_len, kv_dev * HD).astype(jnp.bfloat16),
            "seq",
            scatter_dimension=0,
            tiled=True,
        ).astype(jnp.float32),
    )
    key_parts, val_parts = (
        lax.all_gather(key_sum.astype(bf16), "tp", axis=1, tiled=True),
        lax.all_gather(val_sum.astype(bf16), "tp", axis=1, tiled=True),
    )
    key_grad = jnp.sum(
        key_parts.astype(f32).reshape(local_len, n_tp // ratio, ratio, kv_dev * HD), axis=2
    )
    val_grad = jnp.sum(
        val_parts.astype(f32).reshape(local_len, n_tp // ratio, ratio, kv_dev * HD), axis=2
    )
    grad_kv = jnp.concatenate(
        [key_grad.reshape(local_len, KVH * HD), val_grad.reshape(local_len, KVH * HD)], axis=1
    ).astype(bf16)
    base = lax.dot_general(
        grad_query, query_full, (((1,), (1,)), ((), ())), preferred_element_type=f32
    )
    side = lax.dot_general(grad_kv, w_kv, (((1,), (1,)), ((), ())), preferred_element_type=f32)
    current = lax.dynamic_slice_in_dim(base, tp_index * feat_block, feat_block, 1)
    input_term = lax.dynamic_update_slice_in_dim(base, current + side, tp_index * feat_block, 1)
    grad_normed = lax.psum_scatter(
        input_term.astype(jnp.bfloat16), "tp", scatter_dimension=1, tiled=True
    ).astype(jnp.float32)
    scaled = grad_normed * norm_gain[None, :]
    inner_part = jnp.sum(scaled * mixed_in, axis=1)
    inner = lax.psum(inner_part, "tp") / (feat_block * n_tp)
    grad_in = inv_rms[:, None] * scaled - mixed_in * (inv_rms**3 * inner)[:, None]
    grad_streams = (
        carry[None, :, None] * error[:, None, :] + hc_read[None, :, None] * grad_in[:, None, :]
    )
    return (grad_streams.astype(bf16)[None], loss_value)


def solution(mesh):
    placed = (
        P("role", "seq", "tp"),
        P("tp"),
        P("tp", "seq"),
        P("role", "seq", None, "tp"),
        P(),
        P(),
        P(),
        P("tp"),
        P("seq", "tp"),
        P("tp", None),
        P("tp", "seq"),
    )
    return jax.shard_map(
        per_device,
        mesh=mesh,
        in_specs=placed,
        out_specs=(P("role", "seq", None, "tp"), P()),
        check_vma=False,
    )
```

profile of v0, /device:TPU:0, one launch (start us, length us, event | category | flops | bytes accessed | tf_op | source)
XLA Modules:
  0.0 846.5 jit_solution(5870552372224750379)
XLA Ops:
  7.2 2.1 fusion.7
  9.3 0.7 reduce_sum.89
  10.0 14.3 %fusion.5 = (f32[512,1024]{1,0:T(8,128)}, f32[512,1024]{1,0:T(8,128)S(1)}) fusion(bf16[1,512,4,1024]{3,2,1,0:T(4,128)(2,1)} %param.14, f32[4]{0:T(128)S(1)} %reduce_sum.89, f32[4]{0:T(128)} %param.15), kind=kLoop, calls=%fused_computation.9 | loop fusion | flops 9437184 | bytes 8388640 | tf_op jit(solution)/shard_map/reduce_sum | solution.py:90
  24.5 8.8 %all-reduce = (f32[512]{0:T(512)S(1)}, f32[512]{0:T(512)S(1)}) all-reduce(f32[512]{0:T(512)S(1)} %multiply_reduce_fusion.3, f32[512]{0:T(512)S(1)} %fusion.7), channel_id=1, replica_groups=mesh['role'=4,'seq'=2,'tp'=4] {'tp'}, use_global_device_ids=true, to_apply=%region_5.0 | all-reduce | flops 1024 | bytes 8192 | tf_op jit(solution)/shard_map/psum | solution.py:36
  34.7 6.2 convolution_convert_fusion.2
  41.0 0.7 all-gather.8.cloned.1.call-update
  44.1 48.7 %all-reduce.3.cloned.1.call-done = bf16[512,2048]{1,0:T(8,128)(2,1)} async-done(((bf16[512,2048]{1,0:T(8,128)(2,1)}), bf16[512,2048]{1,0:T(8,128)(2,1)}) %all-reduce.3.cloned.1.call-update) | async-done | bytes 2097168 | tf_op jit(solution)/shard_map/psum | solution.py:57
  92.8 1.1 constant_dynamic-slice_fusion.1
  93.9 8.7 %all_gather.27 = bf16[1024,256]{1,0:T(8,128)(2,1)S(1)} all-gather(bf16[512,256]{1,0:T(8,128)(2,1)S(1)} %get-tuple-element.8), channel_id=1, replica_groups=mesh['role'=4,'seq'=2,'tp'=4] {'seq'}, dimensions={0}, use_global_device_ids=true | all-gather | bytes 786432 | tf_op jit(solution)/shard_map/all_gather | solution.py:64
  102.5 0.9 reshape.67
  103.5 7.8 all_gather.28
  111.8 17.3 %all-gather.8.cloned.1.call-done = bf16[512,4096]{1,0:T(8,128)(2,1)} async-done(((bf16[512,1024]{1,0:T(8,128)(2,1)}), bf16[512,4096]{1,0:T(8,128)(2,1)}) %all-gather.8.cloned.1.call-update) | async-done | bytes 4194320 | tf_op jit(solution)/shard_map/all_gather | solution.py:60
  129.0 105.7 %all-gather.10.cloned.1.call-done = bf16[4096,1024]{1,0:T(8,128)(2,1)} async-done(((bf16[2048,1024]{1,0:T(8,128)(2,1)}), bf16[4096,1024]{1,0:T(8,128)(2,1)}) %all-gather.10.cloned.1.call-update) | async-done | bytes 8388624 | tf_op jit(solution)/shard_map/all_gather | solution.py:55
  234.7 9.1 %convolution_convert_fusion.4 = bf16[512,1024]{1,0:T(8,128)(2,1)S(1)} fusion(bf16[512,4096]{1,0:T(8,128)(2,1)} %all-gather.8.cloned.1.call-done, bf16[4096,1024]{1,0:T(8,128)(2,1)} %all-gather.10.cloned.1.call-done), kind=kOutput, calls=%fused_computation.44 | convolution fusion | flops 4295491584 | bytes 13631488 | tf_op jit(solution)/shard_map/dot_general | solution.py:61
  244.4 4.6 fusion.4
  249.1 7.0 copy-done.27
  256.0 4.4 fusion.24
  260.5 79.8 %all-gather.12.cloned.1.call-done = bf16[1024,4096]{1,0:T(8,128)(2,1)} async-done(((bf16[1024,2048]{1,0:T(8,128)(2,1)}), bf16[1024,4096]{1,0:T(8,128)(2,1)}) %all-gather.12.cloned.1.call-update) | async-done | bytes 8388624 | tf_op jit(solution)/shard_map/all_gather | solution.py:83
  340.2 9.7 %convolution_convert_fusion.1 = bf16[512,4096]{1,0:T(8,128)(2,1)} fusion(bf16[512,1024]{0,1:T(8,128)(2,1)S(1)} %bitcast.91, bf16[1024,4096]{1,0:T(8,128)(2,1)} %all-gather.12.cloned.1.call-done), kind=kOutput, calls=%fused_computation.13 | convolution fusion | flops 4297064448 | bytes 13631488 | tf_op jit(solution)/shard_map/dot_general | solution.py:84
  350.0 190.6 %all-gather.14.cloned.1.call-done = bf16[2048,4096]{1,0:T(8,128)(2,1)} async-done(((bf16[2048,2048]{1,0:T(8,128)(2,1)}), bf16[2048,4096]{1,0:T(8,128)(2,1)}) %all-gather.14.cloned.1.call-update) | async-done | bytes 16777232 | tf_op jit(solution)/shard_map/all_gather | solution.py:42
  540.6 13.8 %convolution_convert_fusion = bf16[512,4096]{1,0:T(8,128)(2,1)} fusion(bf16[2048,4096]{1,0:T(8,128)(2,1)} %all-gather.14.cloned.1.call-done, bf16[1,512,2048]{2,1,0:T(8,128)(2,1)S(1)} %copy-done.11, f32[2048]{0:T(1024)S(1)} %copy-done.25, f32[512]{0:T(512)S(1)} %add_rsqrt_fusion), kind=kOutput, calls=%fused_computation.12 | convolution fusion | flops 8596226048 | bytes 23078912 | tf_op jit(solution)/shard_map/dot_general | solution.py:43
  555.7 32.0 %reduce-scatter.6.cloned.1.call-done = bf16[512,1024]{1,0:T(8,128)(2,1)} async-done(((bf16[512,4096]{1,0:T(8,128)(2,1)}), bf16[512,1024]{1,0:T(8,128)(2,1)}) %reduce-scatter.6.cloned.1.call-update) | async-done | bytes 1048592 | tf_op jit(solution)/shard_map/reduce_scatter | solution.py:85
  587.7 47.7 %reduce-scatter.8.cloned.1.call-done = bf16[512,1024]{1,0:T(8,128)(2,1)} async-done(((bf16[512,4096]{1,0:T(8,128)(2,1)}), bf16[512,1024]{1,0:T(8,128)(2,1)}) %reduce-scatter.8.cloned.1.call-update) | async-done | bytes 1048592 | tf_op jit(solution)/shard_map/reduce_scatter | solution.py:44
  635.4 3.5 multiply_reduce_fusion.1
  638.9 1.3 copy-done.3
  640.2 1.9 multiply_convert_fusion.1
  642.1 34.6 %all-gather.16.cloned.1.call-done = bf16[512,4096]{1,0:T(8,128)(2,1)} async-done(((bf16[512,1024]{1,0:T(8,128)(2,1)}), bf16[512,4096]{1,0:T(8,128)(2,1)}) %all-gather.16.cloned.1.call-update) | async-done | bytes 4194320 | tf_op jit(solution)/shard_map/all_gather | solution.py:95
  676.7 9.2 %convolution_convert_fusion.3 = bf16[512,1024]{1,0:T(8,128)(2,1)S(1)} fusion(bf16[512,4096]{1,0:T(8,128)(2,1)} %all-gather.16.cloned.1.call-done, bf16[1024,4096]{1,0:T(8,128)(2,1)} %all-gather.12.cloned.1.call-done), kind=kOutput, calls=%fused_computation.43 | convolution fusion | flops 4295491584 | bytes 13631488 | tf_op jit(solution)/shard_map/dot_general | solution.py:96
  685.9 1.0 reshape.71
  686.9 1.7 copy.23
  688.9 9.2 %fusion.32 = bf16[2,128,1024]{2,1,0:T(8,128)(2,1)} fusion(bf16[512,2,4,128]{0,3,2,1:T(8,128)(2,1)} %copy.23, f32[2,1024,512,4]{2,1,3,0:T(8,128)} %copy-done.27, f32[2,4,512]{2,1,0:T(4,128)S(1)} %get-tuple-element.10, pred[512,1024]{0,1:T(8,128)(4,1)} %copy-done.14), kind=kOutput, calls=%fused_computation.50 | convolution fusion | flops 1090781184 | bytes 18890752 | tf_op jit(solution)/shard_map/gjqk,qgjd->kgd/dot_general | solution.py:111
  698.2 2.0 copy.34
  700.2 1.9 multiply_reduce_fusion
  702.2 9.3 %fusion.1 = bf16[2,4,512,1024]{2,3,1,0:T(8,128)(2,1)S(1)} fusion(f32[2,4,512]{2,1,0:T(4,128)S(1)} %multiply_reduce_fusion, bf16[512,2,4,128]{0,3,2,1:T(8,128)(2,1)} %copy.23, bf16[1024,2,128,1]{2,1,0,3:T(2,128)(2,1)} %bitcast.93, f32[2,4,512]{2,1,0:T(4,128)S(1)} %get-tuple-element.10, f32[2,1024,512,4]{2,1,3,0:T(8,128)} %copy-done.27, ...), kind=kOutput, calls=%fused_computation.2 | convolution fusion | flops 1098907648 | bytes 27295744 | tf_op jit(solution)/shard_map/qgjd,kgd->gjqk/dot_general | solution.py:101
  711.6 3.6 fusion.31
  716.0 14.1 %reduce-scatter.10.cloned.1.call-done = bf16[512,256]{0,1:T(8,128)(2,1)} async-done(((bf16[1024,256]{0,1:T(8,128)(2,1)}), bf16[512,256]{0,1:T(8,128)(2,1)}) %reduce-scatter.10.cloned.1.call-update) | async-done | bytes 262160 | tf_op jit(solution)/shard_map/reduce_scatter | solution.py:113
  730.2 4.7 multiply_convert_fusion
  734.9 10.6 %fusion.41 = f32[512,4096]{1,0:T(8,128)} fusion(bf16[512,1024]{0,1:T(8,128)(2,1)S(1)} %bitcast.92, bf16[4096,1024]{1,0:T(8,128)(2,1)} %all-gather.10.cloned.1.call-done), kind=kOutput, calls=%fused_computation.62 | convolution fusion | flops 4294967296 | bytes 17825792 | tf_op jit(solution)/shard_map/dot_general | solution.py:139
  745.5 3.0 all-gather.20.cloned.1.call-done
  748.5 18.3 %all-gather.18.cloned.1.call-done = bf16[512,1024]{0,1:T(8,128)(2,1)} async-done(((bf16[512,256]{0,1:T(8,128)(2,1)}), bf16[512,1024]{0,1:T(8,128)(2,1)}) %all-gather.18.cloned.1.call-update) | async-done | bytes 1048592 | tf_op jit(solution)/shard_map/all_gather | solution.py:127
  766.7 7.1 add_dynamic-update-slice_fusion
  773.9 6.0 convert_element_type.129
  779.9 40.0 %psum.39 = f32[]{:T(128)} all-reduce(f32[]{:T(128)} %get-tuple-element.6), channel_id=1, replica_groups=mesh['role'=4,'seq'=2,'tp'=4] {'role','seq','tp'}, use_global_device_ids=true, to_apply=%region_18.19 | all-reduce | flops 1 | bytes 8 | tf_op jit(solution)/shard_map/psum | solution.py:92
  820.6 4.8 reduce-scatter.14.cloned.1.call-done
  825.3 1.6 multiply_reduce_fusion.2
  826.9 5.8 psum.38
  832.7 1.7 multiply_subtract_fusion
  834.6 3.8 add_convert_fusion
  (92 shorter events, 7.8 us)
Async XLA Ops:
  7.2 85.6 %all-reduce.3.cloned.1.call-start = ((), (), s32[]{:S(2)}) async-start(), calls=%async_computation.5 | async-start | bytes 4194304 | tf_op jit(solution)/shard_map/psum | solution.py:57
  10.0 14.3 %copy-start.22 = (f32[4]{0:T(128)}, f32[4]{0:T(128)S(1)}, u32[]{:S(2)}) copy-start(f32[4]{0:T(128)S(1)} %reduce_sum.89) | copy-start | bytes 52
  10.0 24.5 %copy-start.16 = (f32[1024]{0:T(1024)S(1)}, f32[1024]{0:T(1024)}, u32[]{:S(2)}) copy-start(f32[1024]{0:T(1024)} %param.18) | copy-start | bytes 12292
  24.3 16.7 %copy-start = (f32[512,1024]{1,0:T(8,128)}, f32[512,1024]{1,0:T(8,128)S(1)}, u32[]{:S(2)}) copy-start(f32[512,1024]{1,0:T(8,128)S(1)} %get-tuple-element.3) | copy-start | bytes 6291460
  33.3 0.6 copy-start.20
  33.9 0.6 copy-start.18
  34.7 6.2 copy-start.8
  41.0 88.1 %all-gather.8.cloned.1.call-start = ((), (), s32[]{:S(2)}) async-start(), calls=%async_computation.6 | async-start | bytes 5242880 | tf_op jit(solution)/shard_map/all_gather | solution.py:60
  41.7 193.0 %all-gather.10.cloned.1.call-start = ((), (), s32[]{:S(2)}) async-start(), calls=%async_computation.7 | async-start | bytes 12582912 | tf_op jit(solution)/shard_map/all_gather | solution.py:55
  42.4 297.8 %all-gather.12.cloned.1.call-start = ((), (), s32[]{:S(2)}) async-start(), calls=%async_computation.8 | async-start | bytes 12582912 | tf_op jit(solution)/shard_map/all_gather | solution.py:83
  43.0 497.6 %all-gather.14.cloned.1.call-start = ((), (), s32[]{:S(2)}) async-start(), calls=%async_computation.10 | async-start | bytes 25165824 | tf_op jit(solution)/shard_map/all_gather | solution.py:42
  43.6 544.1 %reduce-scatter.6.cloned.1.call-start = ((), (), s32[]{:S(2)}) async-start(), calls=%async_computation.9 | async-start | bytes 5242880 | tf_op jit(solution)/shard_map/reduce_scatter | solution.py:85
  44.1 205.0 %copy-start.14 = (pred[512,1024]{0,1:T(8,128)(4,1)}, pred[512,1024]{0,1:T(8,128)(4,1)S(1)}, u32[]{:S(2)}) copy-start(pred[512,1024]{0,1:T(8,128)(4,1)S(1)} %iota_compare_fusion) | copy-start | bytes 1572868
  111.8 132.7 %copy-start.9 = (bf16[1024,2,128,1]{0,2,3,1:T(8,128)(2,1)}, bf16[1024,2,128,1]{0,2,3,1:T(8,128)(2,1)S(1)}, u32[]{:S(2)}) copy-start(bf16[1024,2,128,1]{0,2,3,1:T(8,128)(2,1)S(1)} %copy.35) | copy-start | bytes 1572868
  244.4 4.7 copy-start.6
  244.4 11.6 %copy-start.15 = (bf16[1024,2,128]{2,1,0:T(2,128)(2,1)S(1)}, bf16[1024,2,128]{2,1,0:T(2,128)(2,1)}, u32[]{:S(2)}) copy-start(bf16[1024,2,128]{2,1,0:T(2,128)(2,1)} %reshape.67) | copy-start | bytes 1572868
  249.1 7.0 copy-start.27
  260.5 79.8 %copy-start.12 = (bf16[2,128,4,512]{3,1,2,0:T(8,128)(2,1)}, bf16[2,128,4,512]{3,1,2,0:T(8,128)(2,1)S(1)}, u32[]{:S(2)}) copy-start(bf16[2,128,4,512]{3,1,2,0:T(8,128)(2,1)S(1)} %fusion.24) | copy-start | bytes 3145732
  349.9 190.7 %copy-start.11 = (bf16[1,512,2048]{2,1,0:T(8,128)(2,1)S(1)}, bf16[1,512,2048]{2,1,0:T(8,128)(2,1)}, u32[]{:S(2)}) copy-start(bf16[1,512,2048]{2,1,0:T(8,128)(2,1)} %param.11) | copy-start | bytes 6291460
  349.9 190.7 %copy-start.25 = (f32[2048]{0:T(1024)S(1)}, f32[2048]{0:T(1024)}, u32[]{:S(2)}) copy-start(f32[2048]{0:T(1024)} %param.12) | copy-start | bytes 24580
  350.0 285.4 %reduce-scatter.8.cloned.1.call-start = ((), (), s32[]{:S(2)}) async-start(), calls=%async_computation.11 | async-start | bytes 5242880 | tf_op jit(solution)/shard_map/reduce_scatter | solution.py:44
  554.4 0.7 copy-start.26
  554.4 81.0 %copy-start.5 = (f32[512,1024]{1,0:T(8,128)S(1)}, f32[512,1024]{1,0:T(8,128)}, u32[]{:S(2)}) copy-start(f32[512,1024]{1,0:T(8,128)} %get-tuple-element.2) | copy-start | bytes 6291460
  554.4 122.3 %all-gather.16.cloned.1.call-start = ((), (), s32[]{:S(2)}) async-start(), calls=%async_computation.12 | async-start | bytes 5242880 | tf_op jit(solution)/shard_map/all_gather | solution.py:95
  638.9 1.3 copy-start.3
  642.1 73.2 %reduce-scatter.12.cloned.1.call-start = ((), (), s32[]{:S(2)}) async-start(), calls=%async_computation.15 | async-start | bytes 786432 | tf_op jit(solution)/shard_map/reduce_scatter | solution.py:119
  698.1 2.1 copy-start.13
  698.1 32.0 %reduce-scatter.10.cloned.1.call-start = ((), (), s32[]{:S(2)}) async-start(), calls=%async_computation.13 | async-start | bytes 786432 | tf_op jit(solution)/shard_map/reduce_scatter | solution.py:113
  702.2 9.4 %copy-start.7 = (bf16[512,1024]{0,1:T(8,128)(2,1)S(1)}, bf16[512,1024]{0,1:T(8,128)(2,1)}, u32[]{:S(2)}) copy-start(bf16[512,1024]{0,1:T(8,128)(2,1)} %copy-done.6) | copy-start | bytes 3145732
  711.5 3.6 copy-start.2
  711.6 18.6 %copy-start.10 = (bf16[1024,2,128,1]{0,2,3,1:T(8,128)(2,1)S(1)}, bf16[1024,2,128,1]{0,2,3,1:T(8,128)(2,1)}, u32[]{:S(2)}) copy-start(bf16[1024,2,128,1]{0,2,3,1:T(8,128)(2,1)} %copy-done.9) | copy-start | bytes 1572868
  715.2 33.3 %all-gather.20.cloned.1.call-start = ((), (), s32[]{:S(2)}) async-start(), calls=%async_computation.16 | async-start | bytes 1310720 | tf_op jit(solution)/shard_map/all_gather | solution.py:128
  715.9 50.8 %all-gather.18.cloned.1.call-start = ((), (), s32[]{:S(2)}) async-start(), calls=%async_computation.14 | async-start | bytes 1310720 | tf_op jit(solution)/shard_map/all_gather | solution.py:127
  730.1 95.2 %reduce-scatter.14.cloned.1.call-start = ((), (), s32[]{:S(2)}) async-start(), calls=%async_computation.17 | async-start | bytes 5242880 | tf_op jit(solution)/shard_map/reduce_scatter | solution.py:145
  779.9 45.4 %copy-start.1 = (f32[512,1024]{1,0:T(8,128)S(1)}, f32[512,1024]{1,0:T(8,128)}, u32[]{:S(2)}) copy-start(f32[512,1024]{1,0:T(8,128)} %copy-done) | copy-start | bytes 6291460
  779.9 45.4 %copy-start.17 = (f32[1024]{0:T(1024)S(1)}, f32[1024]{0:T(1024)}, u32[]{:S(2)}) copy-start(f32[1024]{0:T(1024)} %param.18) | copy-start | bytes 12292
  779.9 52.8 %copy-start.21 = (f32[512]{0:T(512)S(1)}, f32[512]{0:T(512)}, u32[]{:S(2)}) copy-start(f32[512]{0:T(512)} %copy-done.20) | copy-start | bytes 6148
  779.9 52.8 %copy-start.19 = (f32[512]{0:T(512)S(1)}, f32[512]{0:T(512)}, u32[]{:S(2)}) copy-start(f32[512]{0:T(512)} %copy-done.18) | copy-start | bytes 6148
  820.5 13.9 %copy-start.23 = (f32[4]{0:T(128)S(1)}, f32[4]{0:T(128)}, u32[]{:S(2)}) copy-start(f32[4]{0:T(128)} %copy-done.22) | copy-start | bytes 52
  820.5 13.9 %copy-start.24 = (f32[4]{0:T(128)S(1)}, f32[4]{0:T(128)}, u32[]{:S(2)}) copy-start(f32[4]{0:T(128)} %param.15) | copy-start | bytes 52
  832.7 1.9 copy-start.4
Sparse Core Ops, SparseCore 0:
  41.1 51.6 all-reduce.2
  94.4 34.5 all-gather.7
  130.7 104.0 all-gather.9
  236.2 103.9 all-gather.11
  341.7 198.8 all-gather.13
  543.1 44.5 reduce-scatter.5
  590.8 44.5 reduce-scatter.7
  642.2 34.4 all-gather.15
  698.3 14.5 reduce-scatter.11
  715.5 14.5 reduce-scatter.9
  731.7 16.7 all-gather.19
  750.0 16.7 all-gather.17
  780.0 45.2 reduce-scatter.13
where the time goes:
time: 855 us; the launch traced here: 846 us
  waiting for transfers between devices  600 us (70%)
  matrix products  102 us (12%)
  blocking collectives  70.9 us (8%)
  other arithmetic  39.2 us (5%)
  local copies, waits for them, and re-layouts  18 us (2%)
  between operations  16.5 us (2%)
    all_gather x1, waiting for transfers between devices, per_device(): proj_full = lax.all_gather(proj, 'seq', axis=1, tiled=True)  191 us
    all_gather x1, waiting for transfers between devices, per_device(): query_full = lax.all_gather(w_query, 'seq', axis=0, tiled=True)  106 us
    all_gather x1, waiting for transfers between devices, per_device(): out_full = lax.all_gather(w_out, 'seq', axis=1, tiled=True)  79.8 us
    psum x1, waiting for transfers between devices, per_device(): lax.psum(kv_part.astype(jnp.bfloat16), 'tp').astype(jnp.float32)  48.7 us
    reduce_scatter x1, waiting for transfers between devices, per_device(): lax.psum_scatter(target_term.astype(jnp.bfloat16), 'tp', scatter_dimensio...  47.7 us
    psum x1, blocking collectives, per_device(): loss_total = lax.psum(jnp.sum(error * error), ('role', 'seq', 'tp'))  40 us
    all_gather x1, waiting for transfers between devices, per_device(): grad_full = lax.all_gather(grad_out, 'tp', axis=1, tiled=True)  34.6 us
    reduce_scatter x1, waiting for transfers between devices, per_device(): lax.psum_scatter(out_term.astype(jnp.bfloat16), 'tp', scatter_dimension=1...  32 us
  transfers between devices with their start and end apart: 13, of which 12 were waited for; matrix products, arithmetic and copies ran while one was open for 9% of the time, Pallas kernels for 0%

commit v1 on v0

--- a/solution.py
+++ b/solution.py
@@ -1,6 +1,8 @@
 import jax
 import jax.numpy as jnp
 from jax import lax
+from jax.experimental import pallas as pl
+from jax.experimental.pallas import tpu as pltpu
 from jax.sharding import PartitionSpec as P
 
 HEADS = 32
@@ -11,7 +13,7 @@
 epsilon = 1e-05
 
 
-def per_device(
+def per_device_rows(
     teacher_rows,
     teacher_gain,
     proj,
@@ -155,6 +157,242 @@
     return (grad_streams.astype(bf16)[None], loss_value)
 
 
+BLOCK = 256
+
+
+def dot_rows(left, right):
+    return lax.dot_general(left, right, (((1,), (1,)), ((), ())), preferred_element_type=jnp.float32)
+
+
+def dot_cols(left, right):
+    return lax.dot_general(left, right, (((0,), (0,)), ((), ())), preferred_element_type=jnp.float32)
+
+
+def block_probs(query, keys, start):
+    rows, width = query.shape[0], keys.shape[0]
+    expo = jnp.exp(dot_rows(query, keys) * HD ** (-0.5))
+    row = start + lax.broadcasted_iota(jnp.int32, (rows, width), 0)
+    col = lax.broadcasted_iota(jnp.int32, (rows, width), 1)
+    expo = jnp.where(col <= row, expo, 0.0)
+    return expo / jnp.sum(expo, axis=1, keepdims=True)
+
+
+def attend_kernel(query_ref, keys_ref, vals_ref, out_ref):
+    for start in range(0, query_ref.shape[0], BLOCK):
+        stop = start + BLOCK
+        probs = block_probs(query_ref[start:stop, :], keys_ref[:stop, :], start)
+        out_ref[start:stop, :] = jnp.dot(
+            probs.astype(jnp.bfloat16), vals_ref[:stop, :], preferred_element_type=jnp.float32
+        ).astype(jnp.bfloat16)
+
+
+def attend(query, keys, vals):
+    length, width = query.shape
+    heads = pl.BlockSpec((length, HD), lambda h: (0, h))
+    whole = pl.BlockSpec((length, HD), lambda h: (0, 0))
+    return pl.pallas_call(
+        attend_kernel,
+        grid=(width // HD,),
+        in_specs=[heads, whole, whole],
+        out_specs=heads,
+        out_shape=jax.ShapeDtypeStruct((length, width), jnp.bfloat16),
+        compiler_params=pltpu.CompilerParams(vmem_limit_bytes=32 * 2**20),
+        cost_estimate=pl.CostEstimate(
+            flops=length * length * width * 3, bytes_accessed=length * width * 4, transcendentals=0
+        ),
+        name="attend",
+    )(query, keys, vals)
+
+
+def attend_grad_kernel(query_ref, keys_ref, vals_ref, att_ref, grad_ref, gq_ref, gk_ref, gv_ref):
+    @pl.when(pl.program_id(0) == 0)
+    def _():
+        gk_ref[...] = jnp.zeros_like(gk_ref)
+        gv_ref[...] = jnp.zeros_like(gv_ref)
+
+    scale = HD ** (-0.5)
+    for start in range(0, query_ref.shape[0], BLOCK):
+        stop = start + BLOCK
+        query = query_ref[start:stop, :]
+        keys = keys_ref[:stop, :]
+        grad = grad_ref[start:stop, :]
+        probs = block_probs(query, keys, start)
+        delta = jnp.sum(
+            grad.astype(jnp.float32) * att_ref[start:stop, :].astype(jnp.float32),
+            axis=1,
+            keepdims=True,
+        )
+        grad_scores = (probs * (dot_rows(grad, vals_ref[:stop, :]) - delta)).astype(jnp.bfloat16)
+        gq_ref[start:stop, :] = (
+            jnp.dot(grad_scores, keys, preferred_element_type=jnp.float32) * scale
+        ).astype(jnp.bfloat16)
+        gk_ref[:stop, :] += dot_cols(grad_scores, query) * scale
+        gv_ref[:stop, :] += dot_cols(probs.astype(jnp.bfloat16), grad)
+
+
+def attend_grad(query, keys, vals, att, grad):
+    length, width = query.shape
+    heads = pl.BlockSpec((length, HD), lambda h: (0, h))
+    whole = pl.BlockSpec((length, HD), lambda h: (0, 0))
+    kv_shape = jax.ShapeDtypeStruct((length, HD), jnp.float32)
+    return pl.pallas_call(
+        attend_grad_kernel,
+        grid=(width // HD,),
+        in_specs=[heads, whole, whole, heads, heads],
+        out_specs=[heads, whole, whole],
+        out_shape=[jax.ShapeDtypeStruct((length, width), jnp.bfloat16), kv_shape, kv_shape],
+        compiler_params=pltpu.CompilerParams(vmem_limit_bytes=32 * 2**20),
+        cost_estimate=pl.CostEstimate(
+            flops=length * length * width * 6, bytes_accessed=length * width * 8, transcendentals=0
+        ),
+        name="attend_grad",
+    )(query, keys, vals, att, grad)
+
+
+def per_device_heads(
+    teacher_rows,
+    teacher_gain,
+    proj,
+    streams,
+    hc_read,
+    hc_mix,
+    hc_write,
+    norm_gain,
+    w_query,
+    w_kv,
+    w_out,
+):
+    f32 = jnp.float32
+    bf16 = jnp.bfloat16
+    n_seq = lax.axis_size("seq")
+    n_tp = lax.axis_size("tp")
+    s = lax.axis_index("seq")
+    per = n_tp // n_seq
+    length = teacher_rows.shape[1]
+    whole_len = length * n_seq
+    feat = streams.shape[3]
+    features = feat * n_tp
+    swap_pairs = [(0, 1), (1, 0)]
+    turn_pairs = [
+        (a * n_tp + t, (t // per) * n_tp + a * per + t % per)
+        for a in range(n_seq)
+        for t in range(n_tp)
+    ]
+
+    def swap(array):
+        return lax.ppermute(array, "seq", swap_pairs)
+
+    def turn(array):
+        return lax.ppermute(array, ("seq", "tp"), turn_pairs)
+
+    def half(array, index, axis):
+        size = array.shape[axis] // n_seq
+        return lax.dynamic_slice_in_dim(array, index * size, size, axis)
+
+    def gather_turned(array):
+        parts = lax.all_gather(array, "tp", axis=0)
+        parts = parts.reshape(n_seq, per, length, feat).transpose(0, 2, 1, 3)
+        return parts.reshape(whole_len, per * feat)
+
+    def scatter_turned(term):
+        parts = term.reshape(n_seq, length, per, feat).transpose(0, 2, 1, 3)
+        parts = parts.reshape(n_tp, length, feat)
+        return lax.psum_scatter(parts, "tp", scatter_dimension=0, tiled=False)
+
+    def by_seq(own, other):
+        return jnp.where(s == 0, own, other), jnp.where(s == 0, other, own)
+
+    hidden = streams[0].astype(f32)
+    mixed_in = jnp.sum(hidden * hc_read[None, :, None], axis=1)
+    scaled_in = (mixed_in * norm_gain[None, :]).astype(bf16)
+    turned_in = turn(scaled_in)
+    rows = gather_turned(turned_in)
+
+    teacher = teacher_rows[0]
+    teacher_f = teacher.astype(f32)
+    teacher_gained = (teacher_f * teacher_gain[None, :]).astype(bf16)
+    sums = jnp.stack([jnp.sum(mixed_in * mixed_in, axis=1), jnp.sum(teacher_f * teacher_f, axis=1)])
+    placed_sums = lax.dynamic_update_slice_in_dim(
+        jnp.zeros((2, whole_len), f32), sums, s * length, 1
+    )
+    sums_all = lax.psum(placed_sums, ("seq", "tp"))
+    inv_rms_all = lax.rsqrt(sums_all[0] / features + epsilon)
+    inv_t_all = lax.rsqrt(sums_all[1] / (teacher.shape[1] * n_tp) + epsilon)
+    inv_rms = lax.dynamic_slice_in_dim(inv_rms_all, s * length, length, 0)
+
+    kv_part = jnp.dot(scaled_in, w_kv, preferred_element_type=f32)
+    kv_heads = KVH // n_tp
+    kv_part = kv_part.astype(bf16).reshape(length, 2, n_tp, kv_heads * HD).transpose(2, 0, 1, 3)
+    kv_sum = lax.psum_scatter(kv_part, "tp", scatter_dimension=0, tiled=False)
+    kv_sum = (kv_sum.astype(f32) * inv_rms[:, None, None]).astype(bf16)
+    kv_own = half(kv_sum, s, 2)
+    kv_other = swap(half(kv_sum, 1 - s, 2))
+    kv_low, kv_high = by_seq(kv_own, kv_other)
+    kv = jnp.concatenate([kv_low, kv_high], axis=0)
+    keys, vals = kv[:, 0], kv[:, 1]
+
+    query_far = jnp.dot(rows, half(w_query, 1 - s, 1), preferred_element_type=f32).astype(bf16)
+    query_got = swap(query_far)
+    query_own = jnp.dot(rows, half(w_query, s, 1), preferred_element_type=f32)
+    query = ((query_own + query_got.astype(f32)) * inv_rms_all[:, None]).astype(bf16)
+
+    teacher_got = swap(teacher_gained)
+    teacher_low, teacher_high = by_seq(teacher_gained, teacher_got)
+    target_term = jnp.dot(
+        jnp.concatenate([teacher_low, teacher_high], axis=0), proj, preferred_element_type=f32
+    )
+    target_term = target_term * inv_t_all[:, None]
+
+    carry = jnp.sum(hc_mix, axis=0)
+    write = jnp.sum(hc_write)
+    carried = turn(jnp.sum(hidden * carry[None, :, None], axis=1).astype(bf16))
+
+    attended = attend(query, keys, vals)
+    attended_got = swap(attended)
+    out_term = jnp.dot(attended, half(w_out, s, 0), preferred_element_type=f32)
+    out_term = out_term + jnp.dot(
+        attended_got, half(w_out, 1 - s, 0), preferred_element_type=f32
+    )
+    term = (write * out_term - target_term).astype(bf16)
+    error = carried.astype(f32) + scatter_turned(term).astype(f32)
+    loss_total = lax.psum(jnp.sum(error * error), ("role", "seq", "tp"))
+    loss_value = loss_total / (lax.axis_size("role") * whole_len * features)
+    grad_full = gather_turned((write * error).astype(bf16))
+    error_back = turn(error.astype(bf16))
+
+    grad_far = dot_rows(grad_full, half(w_out, 1 - s, 0)).astype(bf16)
+    grad_got = swap(grad_far)
+    grad_own = dot_rows(grad_full, half(w_out, s, 0))
+    grad_att = (grad_own + grad_got.astype(f32)).astype(bf16)
+
+    grad_query, grad_keys, grad_vals = attend_grad(query, keys, vals, attended, grad_att)
+    grad_query_got = swap(grad_query)
+    grad_kv = jnp.stack([grad_keys, grad_vals], axis=1).astype(bf16)
+    inner_part = jnp.sum(grad_query.astype(f32) * query.astype(f32), axis=1) + jnp.sum(
+        grad_kv.astype(f32) * kv.astype(f32), axis=(1, 2)
+    )
+    inner_all = lax.psum(inner_part, ("seq", "tp")) / features
+    inner = lax.dynamic_slice_in_dim(inner_all, s * length, length, 0)
+
+    base = dot_rows(grad_query, half(w_query, s, 1))
+    base = base + dot_rows(grad_query_got, half(w_query, 1 - s, 1))
+    base_sum = turn(scatter_turned(base.astype(bf16)))
+
+    grad_kv_got = swap(half(grad_kv, 1 - s, 0))
+    grad_kv_low, grad_kv_high = by_seq(half(grad_kv, s, 0), grad_kv_got)
+    grad_kv_own = jnp.concatenate([grad_kv_low, grad_kv_high], axis=2)
+    grad_kv_all = lax.all_gather(grad_kv_own, "tp", axis=2, tiled=True).reshape(length, -1)
+    side = dot_rows(grad_kv_all, w_kv)
+
+    scaled = (base_sum.astype(f32) + side) * norm_gain[None, :]
+    grad_in = inv_rms[:, None] * scaled - mixed_in * (inv_rms**2 * inner)[:, None]
+    grad_streams = (
+        carry[None, :, None] * error_back.astype(f32)[:, None, :]
+        + hc_read[None, :, None] * grad_in[:, None, :]
+    )
+    return (grad_streams.astype(bf16)[None], loss_value)
+
+
 def solution(mesh):
     placed = (
         P("role", "seq", "tp"),
@@ -169,8 +407,10 @@
         P("tp", None),
         P("tp", "seq"),
     )
+    seq, tp = mesh.shape["seq"], mesh.shape["tp"]
+    by_heads = seq == 2 and tp % seq == 0 and KVH % (seq * tp) == 0
     return jax.shard_map(
-        per_device,
+        per_device_heads if by_heads else per_device_rows,
         mesh=mesh,
         in_specs=placed,
         out_specs=(P("role", "seq", None, "tp"), P()),

time: 855 us -> 578 us (0.68)
  waiting for transfers between devices: 600 us -> 230 us
  starting transfers between devices: 0.52 us -> 60.6 us
  local copies, waits for them, and re-layouts: 18 us -> 60.9 us
  matrix products: 102 us -> 61.8 us
  Pallas kernels: 0 us -> 18.5 us
  blocking collectives: 70.9 us -> 84.6 us
    all_gather x7 -> x3, waiting for transfers between devices: 449 us -> 41.7 us  [the longest x2 41.7 us: gather_turned(): parts = lax.all_gather(array, 'tp', axis=0)]
    ppermute x0 -> x11, waiting for transfers between devices: none -> 79.9 us  [the longest x7 79.9 us: swap(): return lax.ppermute(array, 'seq', swap_pairs)]
    ppermute x0 -> x11, starting transfers between devices: none -> 59.8 us  [the longest x7 39.4 us: swap(): return lax.ppermute(array, 'seq', swap_pairs)]
    psum x1 -> x0, waiting for transfers between devices: 48.7 us -> none  [per_device(): lax.psum(kv_part.astype(jnp.bfloat16), 'tp').astype(jnp.float32)]
    dot_general x13 -> x11, matrix products: 102 us -> 61.8 us  [the longest x1 18.5 us: per_device_heads(): jnp.dot(jnp.concatenate([teacher_low, teacher_high], axis=0), proj, prefe...]
    reshape x6, local copies, waits for them, and re-layouts: 4.72 us -> 38.5 us  [the longest x3 21.1 us: scatter_turned(): parts = term.reshape(n_seq, length, per, feat).transpose(0, 2, 1, 3)]
    psum x3, blocking collectives: 54.5 us -> 84.6 us  [the longest x1 59.1 us: per_device_heads(): loss_total = lax.psum(jnp.sum(error * error), ('role', 'seq', 'tp'))]
    pallas_call x0 -> x2, Pallas kernels: none -> 18.5 us  [the longest x1 11.2 us: attend_grad(): pl.pallas_call(attend_grad_kernel, grid=(width // HD,), in_specs=[heads,...]
  transfers between devices with their start and end apart: 13 -> 17, of which waited for: 12 -> 10; matrix products, arithmetic and copies ran while one was open for 9% -> 9% of each run, Pallas kernels for 0% -> 1%
where the time goes in v1:
time: 578 us; the launch traced here: 567 us
  waiting for transfers between devices  230 us (40%)
  blocking collectives  84.6 us (15%)
  matrix products  61.8 us (11%)
  local copies, waits for them, and re-layouts  60.9 us (11%)
  starting transfers between devices  60.6 us (10%)
  other arithmetic  33.9 us (6%)
  Pallas kernels  18.5 us (3%)
  between operations  16.9 us (3%)
    reduce_scatter x2, waiting for transfers between devices, scatter_turned(): return lax.psum_scatter(parts, 'tp', scatter_dimension=0, tiled=False)  88.1 us
    ppermute x7, waiting for transfers between devices, swap(): return lax.ppermute(array, 'seq', swap_pairs)  79.9 us
    psum x1, blocking collectives, per_device_heads(): loss_total = lax.psum(jnp.sum(error * error), ('role', 'seq', 'tp'))  59.1 us
    all_gather x2, waiting for transfers between devices, gather_turned(): parts = lax.all_gather(array, 'tp', axis=0)  41.7 us
    ppermute x7, starting transfers between devices, swap(): return lax.ppermute(array, 'seq', swap_pairs)  39.4 us
    reshape x3, local copies, waits for them, and re-layouts, scatter_turned(): parts = term.reshape(n_seq, length, per, feat).transpose(0, 2, 1, 3)  21.1 us
    ppermute x4, starting transfers between devices, turn(): return lax.ppermute(array, ('seq', 'tp'), turn_pairs)  20.4 us
    reduce_scatter x1, waiting for transfers between devices, per_device_heads(): kv_sum = lax.psum_scatter(kv_part, 'tp', scatter_dimension=0, tiled=False)  20 us
  transfers between devices with their start and end apart: 17, of which 10 were waited for; matrix products, arithmetic and copies ran while one was open for 9% of the time, Pallas kernels for 1%

profile of v1, /device:TPU:0, one launch (start us, length us, event | category | flops | bytes accessed | tf_op | source)
XLA Modules:
  0.0 566.9 jit_solution(4025349141252314989)
XLA Ops:
  7.9 14.0 %fusion = (bf16[512,1024]{1,0:T(8,128)(2,1)}, f32[512,1024]{1,0:T(8,128)S(1)}) fusion(bf16[1,512,4,1024]{3,2,1,0:T(4,128)(2,1)} %param.14, f32[4]{0:T(128)S(1)} %reduce_sum.81, f32[4]{0:T(128)} %param.15), kind=kLoop, calls=%fused_computation.2 | loop fusion | flops 9437184 | bytes 7340064 | tf_op jit(solution)/shard_map/reduce_sum | solution.py:348
  25.7 6.2 %convolution_convert_fusion = bf16[512,2048]{1,0:T(8,128)(2,1)} fusion(bf16[512,1024]{1,0:T(8,128)(2,1)} %copy-done.14, bf16[1024,2048]{1,0:T(8,128)(2,1)} %param.20), kind=kOutput, calls=%fused_computation.14 | convolution fusion | flops 2148532224 | bytes 7340032 | tf_op jit(solution)/shard_map/dot_general | solution.py:323
  31.9 2.9 copy.17
  34.8 2.4 copy.18
  37.3 2.3 fusion.3
  39.5 30.1 %collective-permute-start.5 = (bf16[512,2048]{1,0:T(8,128)(2,1)S(1)}, bf16[512,2048]{1,0:T(8,128)(2,1)}, u32[]{:S(2)}, u32[]{:S(2)}) collective-permute-start(bf16[512,2048]{1,0:T(8,128)(2,1)S(1)} %get-tuple-element.15), channel_id=1, source_target_pairs={{0,4},{4,0},{1,5},{5,1},{2,6},{6,2},{3,7},{7,3},{8,12},{12,8},{9,1... | collective-permute-start | bytes 6291464 | tf_op jit(solution)/shard_map/ppermute | solution.py:283
  69.6 12.6 %psum.21 = f32[2,1024]{1,0:T(2,128)S(1)} all-reduce(f32[2,1024]{1,0:T(2,128)S(1)} %maximum_dynamic-update-slice_fusion), channel_id=1, replica_groups=mesh['role'=4,'seq'=2,'tp'=4] {'seq','tp'}, use_global_device_ids=true, to_apply=%region_6.7 | all-reduce | flops 2048 | bytes 16384 | tf_op jit(solution)/shard_map/psum | solution.py:318
  82.3 7.0 %all-gather.8.cloned.1.call-done = bf16[2048,1024]{1,0:T(8,128)(2,1)} async-done(((bf16[512,1024]{1,0:T(8,128)(2,1)}), bf16[2048,1024]{1,0:T(8,128)(2,1)}) %all-gather.8.cloned.1.call-update) | async-done | bytes 4194320 | tf_op jit(solution)/shard_map/all_gather | solution.py:293
  89.3 6.5 %copy.15 = bf16[2,2,512,1024]{3,1,2,0:T(2,128)(2,1)S(1)} copy(bf16[2,2,512,1024]{3,2,1,0:T(8,128)(2,1)} %bitcast.68) | data formatting | bytes 8388608 | tf_op jit(solution)/shard_map/reshape | solution.py:294
  98.6 3.3 fusion.23
  103.3 20.0 %reduce-scatter.4.cloned.1.call-done = bf16[1,512,2,256]{3,1,2,0:T(8,128)(2,1)} async-done(((bf16[4,512,2,256]{3,1,2,0:T(8,128)(2,1)}), bf16[1,512,2,256]{3,1,2,0:T(8,128)(2,1)}) %reduce-scatter.4.cloned.1.call-update) | async-done | bytes 524304 | tf_op jit(solution)/shard_map/reduce_scatter | solution.py:326
  124.5 1.6 collective-permute-start.3
  126.7 16.1 %collective-permute-done.3 = bf16[512,2,128]{2,0,1:T(8,128)(2,1)S(1)} collective-permute-done((bf16[512,2,128]{2,0,1:T(8,128)(2,1)S(1)}, bf16[512,2,128]{2,0,1:T(8,128)(2,1)S(1)}, u32[]{:S(2)}, u32[]{:S(2)}) %collective-permute-start.3) | collective-permute-done | bytes 262176 | tf_op jit(solution)/shard_map/ppermute | solution.py:283
  143.7 5.4 multiply_convert_fusion.1.query_ref
  149.1 7.3 %attend.1.att_ref = bf16[1024,512]{1,0:T(8,128)(2,1)S(1)} custom-call(bf16[1024,512]{1,0:T(8,128)(2,1)S(1)} %multiply_convert_fusion.1.query_ref, bf16[1024,128]{1,0:T(8,128)(2,1)S(1)} %get-tuple-element.24.keys_ref, bf16[1024,128]{1,0:T(8,128)(2,1)S(1)} %get-tuple-element.23.vals_ref), custom_call_target="tpu_custom_call" | custom-call | flops 1610612736 | bytes 2097152 | tf_op jit(solution)/shard_map/attend/pallas_call | solution.py:193
  156.4 1.8 collective-permute-start.4
  158.2 1.9 broadcast_select_fusion.1
  160.1 5.6 fusion.14
  165.7 14.1 %collective-permute-done.4 = bf16[1024,512]{1,0:T(8,128)(2,1)S(1)} collective-permute-done((bf16[1024,512]{1,0:T(8,128)(2,1)S(1)}, bf16[1024,512]{1,0:T(8,128)(2,1)S(1)}, u32[]{:S(2)}, u32[]{:S(2)}) %collective-permute-start.4) | collective-permute-done | bytes 1048608 | tf_op jit(solution)/shard_map/ppermute | solution.py:283
  179.8 5.6 fusion.10
  185.4 18.5 %subtract_convert_fusion = bf16[1024,2048]{1,0:T(8,128)(2,1)} fusion(f32[1024,2048]{1,0:T(8,128)} %fusion.14, f32[1024,2048]{1,0:T(8,128)} %fusion.10, bf16[2048,2048]{1,0:T(8,128)(2,1)} %param.13, bf16[512,2048]{1,0:T(8,128)(2,1)S(1)} %get-tuple-element.11, bf16[512,2048]{1,0:T(8,128)(2,1)S(1)} %get-tuple-element.10, f32[1024]{0:T(1024)S(1)} %bitcast.81, ...), kind=kOutput, calls=%fused_computation.6 | convolution fusion | flops 8608808960 | bytes 33558532 | tf_op jit(solution)/shard_map/dot_general | solution.py:341
  203.9 7.8 %reshape.91 = bf16[2,512,2,1024]{3,2,1,0:T(2,128)(2,1)} reshape(bf16[1024,2048]{1,0:T(8,128)(2,1)} %subtract_convert_fusion) | data formatting | bytes 8388608 | tf_op jit(solution)/shard_map/reshape | solution.py:298
  211.7 5.5 copy.19
  219.1 48.0 %reduce-scatter.6.cloned.1.call-done = bf16[1,512,1024]{2,1,0:T(8,128)(2,1)} async-done(((bf16[4,512,1024]{2,1,0:T(8,128)(2,1)}), bf16[1,512,1024]{2,1,0:T(8,128)(2,1)}) %reduce-scatter.6.cloned.1.call-update) | async-done | bytes 1048592 | tf_op jit(solution)/shard_map/reduce_scatter | solution.py:300
  267.2 4.4 multiply_reduce_fusion
  271.8 34.7 %all-gather.10.cloned.1.call-done = bf16[2048,1024]{1,0:T(8,128)(2,1)} async-done(((bf16[512,1024]{1,0:T(8,128)(2,1)}), bf16[2048,1024]{1,0:T(8,128)(2,1)}) %all-gather.10.cloned.1.call-update) | async-done | bytes 4194320 | tf_op jit(solution)/shard_map/all_gather | solution.py:293
  306.5 8.5 %copy.20 = bf16[2,2,512,1024]{3,1,2,0:T(2,128)(2,1)} copy(bf16[2,2,512,1024]{3,2,1,0:T(8,128)(2,1)} %bitcast.71) | data formatting | bytes 8388608 | tf_op jit(solution)/shard_map/reshape | solution.py:294
  315.0 3.8 copy.25
  318.8 2.4 fusion.26
  322.7 23.8 %collective-permute-done.7 = bf16[1024,512]{1,0:T(8,128)(2,1)S(1)} collective-permute-done((bf16[1024,512]{1,0:T(8,128)(2,1)S(1)}, bf16[1024,512]{1,0:T(8,128)(2,1)S(1)}, u32[]{:S(2)}, u32[]{:S(2)}) %collective-permute-start.7) | collective-permute-done | bytes 1048608 | tf_op jit(solution)/shard_map/ppermute | solution.py:283
  346.6 2.4 add_convert_fusion.2.grad_ref
  349.0 11.2 %attend_grad.1 = (bf16[1024,512]{1,0:T(8,128)(2,1)S(1)}, f32[1024,128]{1,0:T(8,128)S(1)}, f32[1024,128]{1,0:T(8,128)S(1)}) custom-call(bf16[1024,512]{1,0:T(8,128)(2,1)S(1)} %multiply_convert_fusion.1.query_ref, bf16[1024,128]{1,0:T(8,128)(2,1)S(1)} %copy-done.1, bf16[1024,128]{1,0:T(8,128)(2,1)S(1)} %get-tuple-element.23.vals_ref, ...), custom_call_target="tpu_custom_call" | custom-call | flops 3221225472 | bytes 4194304 | tf_op jit(solution)/shard_map/attend_grad/pallas_call | solution.py:238
  360.2 1.6 collective-permute-start.8
  361.7 2.4 fusion.19
  364.1 20.6 %collective-permute-done.8 = bf16[1024,512]{1,0:T(8,128)(2,1)S(1)} collective-permute-done((bf16[1024,512]{1,0:T(8,128)(2,1)S(1)}, bf16[1024,512]{1,0:T(8,128)(2,1)S(1)}, u32[]{:S(2)}, u32[]{:S(2)}) %collective-permute-start.8) | collective-permute-done | bytes 1048608 | tf_op jit(solution)/shard_map/ppermute | solution.py:283
  384.7 4.4 add_convert_fusion.1
  389.1 7.8 %reshape.95 = bf16[2,512,2,1024]{3,2,1,0:T(2,128)(2,1)} reshape(bf16[1024,2048]{1,0:T(8,128)(2,1)} %add_convert_fusion.1) | data formatting | bytes 8388608 | tf_op jit(solution)/shard_map/reshape | solution.py:298
  396.9 5.5 copy.21
  404.2 5.3 collective-permute-done.10
  410.5 9.5 %collective-permute-start.6 = (bf16[512,1024]{1,0:T(8,128)(2,1)}, bf16[512,1024]{1,0:T(8,128)(2,1)}, u32[]{:S(2)}, u32[]{:S(2)}) collective-permute-start(bf16[512,1024]{1,0:T(8,128)(2,1)} %get-tuple-element.14), channel_id=1, source_target_pairs={{0,0},{1,1},{2,4},{3,5},{4,2},{5,3},{6,6},{7,7},{8,8},{9,9},{10,12... | collective-permute-start | bytes 3145736 | tf_op jit(solution)/shard_map/ppermute | solution.py:286
  420.0 40.0 %reduce-scatter.8.cloned.1.call-done = bf16[1,512,1024]{2,1,0:T(8,128)(2,1)} async-done(((bf16[4,512,1024]{2,1,0:T(8,128)(2,1)}), bf16[1,512,1024]{2,1,0:T(8,128)(2,1)}) %reduce-scatter.8.cloned.1.call-update) | async-done | bytes 1048592 | tf_op jit(solution)/shard_map/reduce_scatter | solution.py:300
  460.0 9.5 %collective-permute-start.9 = (bf16[512,1024]{1,0:T(8,128)(2,1)}, bf16[512,1024]{1,0:T(8,128)(2,1)}, u32[]{:S(2)}, u32[]{:S(2)}) collective-permute-start(bf16[512,1024]{1,0:T(8,128)(2,1)} %bitcast.82), channel_id=1, source_target_pairs={{0,0},{1,1},{2,4},{3,5},{4,2},{5,3},{6,6},{7,7},{8,8},{9,9},{10,12... | collective-permute-start | bytes 3145736 | tf_op jit(solution)/shard_map/ppermute | solution.py:286
  469.5 59.1 %psum.23 = f32[]{:T(128)} all-reduce(f32[]{:T(128)} %get-tuple-element.12), channel_id=1, replica_groups=mesh['role'=4,'seq'=2,'tp'=4] {'role','seq','tp'}, use_global_device_ids=true, to_apply=%region_14.15 | all-reduce | flops 1 | bytes 8 | tf_op jit(solution)/shard_map/psum | solution.py:358
  529.2 2.8 convert_element_type.120
  532.6 12.9 %psum.22 = f32[1024]{0:T(1024)S(1)} all-reduce(f32[1024]{0:T(1024)S(1)} %add.94), channel_id=1, replica_groups=mesh['role'=4,'seq'=2,'tp'=4] {'seq','tp'}, use_global_device_ids=true, to_apply=%region_12.13 | all-reduce | flops 1024 | bytes 8192 | tf_op jit(solution)/shard_map/psum | solution.py:374
  545.6 3.1 copy.22
  548.8 5.8 %multiply_subtract_fusion = f32[512,1024]{1,0:T(8,128)S(1)} fusion(f32[512,1024]{1,0:T(8,128)} %copy-done.5, bf16[512,1024]{1,0:T(8,128)(2,1)} %collective-permute-done.9, f32[512]{0:T(512)S(1)} %dynamic-slice_multiply_fusion, f32[512]{0:T(512)S(1)} %bitcast.77, f32[1024]{0:T(1024)S(1)} %copy-done.17, bf16[512,2048]{0,1:T(8,128)(2,1)S(1)} %bitcast.74, ...), kind=kOutput, calls=%fused_computation.17 | convolution fusion | flops 2150629376 | bytes 11542528 | tf_op jit(solution)/shard_map/dot_general | solution.py:164
  554.6 3.8 add_convert_fusion
  (93 shorter events, 18.6 us)
Async XLA Ops:
  7.2 14.8 %copy-start.17 = (f32[1024]{0:T(1024)S(1)}, f32[1024]{0:T(1024)}, u32[]{:S(2)}) copy-start(f32[1024]{0:T(1024)} %param.18) | copy-start | bytes 12292
  7.2 82.1 %all-gather.8.cloned.1.call-start = ((), (), s32[]{:S(2)}) async-start(), calls=%async_computation.7 | async-start | bytes 5242880 | tf_op jit(solution)/shard_map/all_gather | solution.py:293
  21.9 3.8 copy-start.5
  22.2 1.3 copy-start.14
  23.5 0.7 collective-permute-start.1
  24.2 1.1 copy-start.13
  25.3 97.9 %reduce-scatter.4.cloned.1.call-start = ((), (), s32[]{:S(2)}) async-start(), calls=%async_computation.3 | async-start | bytes 2621440 | tf_op jit(solution)/shard_map/reduce_scatter | solution.py:326
  34.8 2.5 copy-start.16
  37.2 230.0 %reduce-scatter.6.cloned.1.call-start = ((), (), s32[]{:S(2)}) async-start(), calls=%async_computation.4 | async-start | bytes 5242880 | tf_op jit(solution)/shard_map/reduce_scatter | solution.py:300
  39.5 118.7 %collective-permute-start.5 = (bf16[512,2048]{1,0:T(8,128)(2,1)S(1)}, bf16[512,2048]{1,0:T(8,128)(2,1)}, u32[]{:S(2)}, u32[]{:S(2)}) collective-permute-start(bf16[512,2048]{1,0:T(8,128)(2,1)S(1)} %get-tuple-element.15), channel_id=1, source_target_pairs={{0,4},{4,0},{1,5},{5,1},{2,6},{6,2},{3,7},{7,3},{8,12},{12,8},{9,1... | collective-permute-start | bytes 6291464 | tf_op jit(solution)/shard_map/ppermute | solution.py:283
  95.8 2.8 copy-start.21
  97.3 4.7 copy-start.6
  98.6 27.5 %copy-start.23 = (f32[4]{0:T(128)S(1)}, f32[4]{0:T(128)}, u32[]{:S(2)}) copy-start(f32[4]{0:T(128)} %param.17) | copy-start | bytes 52
  102.0 41.0 %collective-permute-start.2 = (bf16[1024,512]{1,0:T(8,128)(2,1)}, bf16[1024,512]{1,0:T(8,128)(2,1)}, u32[]{:S(2)}, u32[]{:S(2)}) collective-permute-start(bf16[1024,512]{1,0:T(8,128)(2,1)} %fusion.23), channel_id=1, source_target_pairs={{0,4},{4,0},{1,5},{5,1},{2,6},{6,2},{3,7},{7,3},{8,12},{12,8},{9,1... | collective-permute-start | bytes 3145736 | tf_op jit(solution)/shard_map/ppermute | solution.py:283
  124.5 18.2 %collective-permute-start.3 = (bf16[512,2,128]{2,0,1:T(8,128)(2,1)S(1)}, bf16[512,2,128]{2,0,1:T(8,128)(2,1)S(1)}, u32[]{:S(2)}, u32[]{:S(2)}) collective-permute-start(bf16[512,2,128]{2,0,1:T(8,128)(2,1)S(1)} %constant_dynamic-slice_fusion), channel_id=1, source_target_pairs={{0,4},{4,0},{1,5},{5,1},{2,6},{6,2},{3,7},{7,3},{8,12},{12,8},{9,1... | collective-permute-start | bytes 786440 | tf_op jit(solution)/shard_map/ppermute | solution.py:283
  142.9 0.7 copy-start.9
  142.9 0.8 copy-start.11
  142.9 6.1 %copy-start = (bf16[1024,128]{1,0:T(8,128)(2,1)}, bf16[1024,128]{1,0:T(8,128)(2,1)S(1)}, u32[]{:S(2)}) copy-start(bf16[1024,128]{1,0:T(8,128)(2,1)S(1)} %get-tuple-element.24.keys_ref) | copy-start | bytes 786436
  156.4 3.7 copy-start.2
  156.4 3.7 copy-start.19
  156.4 23.4 %collective-permute-start.4 = (bf16[1024,512]{1,0:T(8,128)(2,1)S(1)}, bf16[1024,512]{1,0:T(8,128)(2,1)S(1)}, u32[]{:S(2)}, u32[]{:S(2)}) collective-permute-start(bf16[1024,512]{1,0:T(8,128)(2,1)S(1)} %attend.1.att_ref), channel_id=1, source_target_pairs={{0,4},{4,0},{1,5},{5,1},{2,6},{6,2},{3,7},{7,3},{8,12},{12,8},{9,1... | collective-permute-start | bytes 3145736 | tf_op jit(solution)/shard_map/ppermute | solution.py:283
  217.2 1.2 copy-start.15
  217.2 89.3 %all-gather.10.cloned.1.call-start = ((), (), s32[]{:S(2)}) async-start(), calls=%async_computation.8 | async-start | bytes 5242880 | tf_op jit(solution)/shard_map/all_gather | solution.py:293
  218.4 0.7 collective-permute-start
  271.6 188.4 %reduce-scatter.8.cloned.1.call-start = ((), (), s32[]{:S(2)}) async-start(), calls=%async_computation.5 | async-start | bytes 5242880 | tf_op jit(solution)/shard_map/reduce_scatter | solution.py:300
  315.0 3.8 copy-start.20
  321.2 27.8 %copy-start.1 = (bf16[1024,128]{1,0:T(8,128)(2,1)S(1)}, bf16[1024,128]{1,0:T(8,128)(2,1)}, u32[]{:S(2)}) copy-start(bf16[1024,128]{1,0:T(8,128)(2,1)} %copy-done) | copy-start | bytes 786436
  321.2 27.8 %copy-start.3 = (bf16[1024,512]{1,0:T(8,128)(2,1)S(1)}, bf16[1024,512]{1,0:T(8,128)(2,1)}, u32[]{:S(2)}) copy-start(bf16[1024,512]{1,0:T(8,128)(2,1)} %copy-done.2) | copy-start | bytes 3145732
  321.2 25.4 %collective-permute-start.7 = (bf16[1024,512]{1,0:T(8,128)(2,1)S(1)}, bf16[1024,512]{1,0:T(8,128)(2,1)S(1)}, u32[]{:S(2)}, u32[]{:S(2)}) collective-permute-start(bf16[1024,512]{1,0:T(8,128)(2,1)S(1)} %fusion.26), channel_id=1, source_target_pairs={{0,4},{4,0},{1,5},{5,1},{2,6},{6,2},{3,7},{7,3},{8,12},{12,8},{9,1... | collective-permute-start | bytes 3145736 | tf_op jit(solution)/shard_map/ppermute | solution.py:283
  349.0 12.7 %copy-start.22 = (bf16[2048,1024]{1,0:T(8,128)(2,1)S(1)}, bf16[2048,1024]{1,0:T(8,128)(2,1)}, u32[]{:S(2)}) copy-start(bf16[2048,1024]{1,0:T(8,128)(2,1)} %param.19) | copy-start | bytes 12582916
  360.2 24.6 %collective-permute-start.8 = (bf16[1024,512]{1,0:T(8,128)(2,1)S(1)}, bf16[1024,512]{1,0:T(8,128)(2,1)S(1)}, u32[]{:S(2)}, u32[]{:S(2)}) collective-permute-start(bf16[1024,512]{1,0:T(8,128)(2,1)S(1)} %get-tuple-element.5), channel_id=1, source_target_pairs={{0,4},{4,0},{1,5},{5,1},{2,6},{6,2},{3,7},{7,3},{8,12},{12,8},{9,1... | collective-permute-start | bytes 3145736 | tf_op jit(solution)/shard_map/ppermute | solution.py:283
  402.5 143.1 %all-gather.6.cloned.1.call-start = ((), (), s32[]{:S(2)}) async-start(), calls=%async_computation.6 | async-start | bytes 2621440 | tf_op jit(solution)/shard_map/all_gather | solution.py:384
  402.6 6.9 %copy-start.7 = (bf16[1024,1,128]{2,0,1:T(8,128)(2,1)}, bf16[1024,1,128]{2,0,1:T(8,128)(2,1)S(1)}, u32[]{:S(2)}) copy-start(bf16[1024,1,128]{2,0,1:T(8,128)(2,1)S(1)} %get-tuple-element.28) | copy-start | bytes 786436
  402.6 129.4 %copy-start.10 = (bf16[512,2,128]{2,0,1:T(8,128)(2,1)S(1)}, bf16[512,2,128]{2,0,1:T(8,128)(2,1)}, u32[]{:S(2)}) copy-start(bf16[512,2,128]{2,0,1:T(8,128)(2,1)} %copy-done.9) | copy-start | bytes 786436
  402.6 129.4 %copy-start.12 = (bf16[512,2,128]{2,0,1:T(8,128)(2,1)S(1)}, bf16[512,2,128]{2,0,1:T(8,128)(2,1)}, u32[]{:S(2)}) copy-start(bf16[512,2,128]{2,0,1:T(8,128)(2,1)} %copy-done.11) | copy-start | bytes 786436
  402.7 6.8 %collective-permute-start.10 = (bf16[512,2,128]{2,0,1:T(8,128)(2,1)S(1)}, bf16[512,2,128]{2,0,1:T(8,128)(2,1)S(1)}, u32[]{:S(2)}, u32[]{:S(2)}) collective-permute-start(bf16[512,2,128]{2,0,1:T(8,128)(2,1)S(1)} %fusion.35), channel_id=1, source_target_pairs={{0,4},{4,0},{1,5},{5,1},{2,6},{6,2},{3,7},{7,3},{8,12},{12,8},{9,1... | collective-permute-start | bytes 786440 | tf_op jit(solution)/shard_map/ppermute | solution.py:283
  409.6 122.5 %copy-start.8 = (bf16[1024,1,128]{2,0,1:T(8,128)(2,1)S(1)}, bf16[1024,1,128]{2,0,1:T(8,128)(2,1)}, u32[]{:S(2)}) copy-start(bf16[1024,1,128]{2,0,1:T(8,128)(2,1)} %copy-done.7) | copy-start | bytes 786436
  410.5 118.7 %collective-permute-start.6 = (bf16[512,1024]{1,0:T(8,128)(2,1)}, bf16[512,1024]{1,0:T(8,128)(2,1)}, u32[]{:S(2)}, u32[]{:S(2)}) collective-permute-start(bf16[512,1024]{1,0:T(8,128)(2,1)} %get-tuple-element.14), channel_id=1, source_target_pairs={{0,0},{1,1},{2,4},{3,5},{4,2},{5,3},{6,6},{7,7},{8,8},{9,9},{10,12... | collective-permute-start | bytes 3145736 | tf_op jit(solution)/shard_map/ppermute | solution.py:286
  460.0 88.7 %collective-permute-start.9 = (bf16[512,1024]{1,0:T(8,128)(2,1)}, bf16[512,1024]{1,0:T(8,128)(2,1)}, u32[]{:S(2)}, u32[]{:S(2)}) collective-permute-start(bf16[512,1024]{1,0:T(8,128)(2,1)} %bitcast.82), channel_id=1, source_target_pairs={{0,0},{1,1},{2,4},{3,5},{4,2},{5,3},{6,6},{7,7},{8,8},{9,9},{10,12... | collective-permute-start | bytes 3145736 | tf_op jit(solution)/shard_map/ppermute | solution.py:286
  548.7 5.8 %copy-start.4 = (f32[512,1024]{1,0:T(8,128)S(1)}, f32[512,1024]{1,0:T(8,128)}, u32[]{:S(2)}) copy-start(f32[512,1024]{1,0:T(8,128)} %convert_element_type.120) | copy-start | bytes 6291460
  548.7 5.8 %copy-start.18 = (f32[4]{0:T(128)S(1)}, f32[4]{0:T(128)}, u32[]{:S(2)}) copy-start(f32[4]{0:T(128)} %param.15) | copy-start | bytes 52
Sparse Core Ops, SparseCore 0:
  25.5 63.7 all-gather.7
  91.8 31.4 reduce-scatter.3
  217.3 49.7 reduce-scatter.5
  271.7 34.7 all-gather.9
  402.6 57.3 reduce-scatter.7
  461.5 33.2 all-gather.5
